TPU v7x, 256 devices: a whole 4x4x8 slice. The times are simulated.
256 devices in a mesh: step: 8 (over x_lo, y), ctx: 32 (over x_hi, z, core).
Axes of the slice: x: 4 (x_hi: 2, x_lo: 2; x = x_hi * 2 + x_lo), y: 4, z: 8, core: 2. Of those that a mesh axis runs over, the one named last changes fastest.
Arguments:
- latent: bfloat16 [8, 2048, 4096], P('step', 'ctx'), may hold values from -6 to 6
- span_queries: bfloat16 [8, 2048, 4096], P('step', 'ctx'), may hold values from -8 to 8
- span_keys: bfloat16 [8, 2048, 4096], P('step', 'ctx'), may hold values from -8 to 8
- span_values: bfloat16 [8, 2048, 4096], P('step', 'ctx'), may hold values from -6 to 6
- cache_keys: bfloat16 [4096, 4096], P(None, 'ctx'), may hold values from -6 to 6
- cache_values: bfloat16 [4096, 4096], P(None, 'ctx'), may hold values from -6 to 6
- time_weight: bfloat16 [256, 4096], P(None, 'ctx'), may hold values from -4 to 4
- timestep: int32 [8], replicated, may hold values from 0 to 999, as said below
- span_index: int32 [8], replicated, may hold values from 67 to 80, as said below
- prefix_spans: int32 [8], replicated, may hold values from 1 to 2, as said below
Outputs:
- advanced: bfloat16 [8, 2048, 4096], P('step', 'ctx')
Inputs may be any that keep to these rules, and one draw needn't show every extreme that they name: `timestep`: timesteps fall strictly from group to group; the first group's is 999 and the last group's is 0. `span_index`: span numbers fall from group to group by 2, except at exactly one step where they fall by 1; the first group's is 80. `prefix_spans`: some group sees all 2 cached spans.
All inputs are finite; a program needn't handle non-finite values.
Results may differ from a plain program's by a relative error of at most 0.012.
Values may be sent and summed in bfloat16 or wider, within the bound.
A program may use at most 128 MiB of HBM per device.

v0:
```python
import math

import jax
import jax.numpy as jnp
from jax import lax
from jax.sharding import PartitionSpec as P

HEAD_DIM = 128
FREQS = 256
FRAMES = 3


def from_root(shard, axis, root):
    mine = lax.axis_index(axis) == root
    return lax.psum(jnp.where(mine, shard, jnp.zeros_like(shard)), axis)


def passed_along(block, axis, distance):
    devices = range(lax.axis_size(axis))
    route = [((i - distance) % len(devices), i) for i in devices]
    return lax.ppermute(block, axis, route)


def rotary(field, positions):
    halves = HEAD_DIM // 2
    inverse = 10000.0 ** (-jnp.arange(halves, dtype=jnp.float32) / halves)
    angles = positions[:, None] * inverse[None, :]
    cosine = jnp.cos(angles)[:, None, :]
    sine = jnp.sin(angles)[:, None, :]
    shaped = field.astype(jnp.float32).reshape(field.shape[0], -1, 2, halves)
    first = shaped[:, :, 0]
    second = shaped[:, :, 1]
    turned = jnp.stack([first * cosine - second * sine, second * cosine + first * sine], axis=2)
    return turned.reshape(field.shape).astype(jnp.bfloat16)


def pick_entry(table, which):
    matches = jnp.arange(table.shape[0], dtype=jnp.int32) == which
    return jnp.sum(jnp.where(matches, table, 0))


def time_gate(level, time_weight):
    halves = FREQS // 2
    freqs = 10000.0 ** (-jnp.arange(halves, dtype=jnp.float32) / halves)
    angles = level.astype(jnp.float32) * freqs
    embedded = jnp.concatenate([jnp.cos(angles), jnp.sin(angles)])
    return jnp.dot(embedded, time_weight.astype(jnp.float32), precision=lax.Precision.HIGHEST)


def body(
    latent,
    span_queries,
    span_keys,
    span_values,
    cache_keys,
    cache_values,
    time_weight,
    timestep,
    span_index,
    prefix_spans,
):
    groups_count = lax.axis_size("step")
    group_rank = lax.axis_index("step")
    context_size = lax.axis_size("ctx")
    context_rank = lax.axis_index("ctx")
    tok_rows = latent.shape[1]
    token_total = tok_rows * context_size
    width_local = cache_keys.shape[1]
    local_heads = width_local // HEAD_DIM
    final_group = groups_count - 1
    row_index = context_rank * tok_rows + jnp.arange(tok_rows, dtype=jnp.int32)
    frames = pick_entry(span_index, group_rank) * FRAMES + row_index * FRAMES // token_total
    positions = frames.astype(jnp.float32)
    queries = rotary(span_queries[0], positions)
    own_keys = rotary(span_keys[0], positions)
    own_values = span_values[0]
    head_queries, head_keys, head_values = (
        lax.all_to_all(queries, "ctx", split_axis=1, concat_axis=0, tiled=True),
        lax.all_to_all(own_keys, "ctx", split_axis=1, concat_axis=0, tiled=True),
        lax.all_to_all(own_values, "ctx", split_axis=1, concat_axis=0, tiled=True),
    )
    fresh_keys, fresh_values = (
        from_root(head_keys, "step", final_group),
        from_root(head_values, "step", final_group),
    )
    keys_all = jnp.concatenate([cache_keys, fresh_keys, head_keys], 0).reshape(
        -1, local_heads, HEAD_DIM
    )
    values_all = jnp.concatenate([cache_values, fresh_values, head_values], 0).reshape(
        -1, local_heads, HEAD_DIM
    )
    cache_slots = cache_keys.shape[0] // token_total
    slot = jnp.arange(keys_all.shape[0], dtype=jnp.int32) // token_total
    seen_slots = pick_entry(prefix_spans, group_rank)
    visible = jnp.where(
        slot < cache_slots,
        slot >= cache_slots - seen_slots,
        jnp.where(slot == cache_slots, group_rank != final_group, True),
    )
    gate = time_gate(pick_entry(timestep, group_rank), time_weight)
    block = math.gcd(token_total, 512)
    blocked = head_queries.reshape(token_total // block, block, local_heads, HEAD_DIM)
    scale = 1.0 / math.sqrt(HEAD_DIM)

    def attend_block(query_block):
        scores = (
            jnp.einsum("qhd,khd->hqk", query_block, keys_all, preferred_element_type=jnp.float32)
            * scale
        )
        scores = jnp.where(visible[None, None, :], scores, -jnp.inf)
        peak = jnp.max(scores, axis=2, keepdims=True)
        weights = jnp.exp(scores - peak)
        totals = jnp.sum(weights, axis=2)
        mixed = jnp.einsum(
            "hqk,khd->qhd",
            weights.astype(jnp.bfloat16),
            values_all,
            preferred_element_type=jnp.float32,
        )
        mixed = mixed / jnp.transpose(totals)[:, :, None]
        return (mixed.reshape(block, width_local) * gate[None, :]).astype(jnp.bfloat16)

    gated = lax.map(attend_block, blocked).reshape(token_total, width_local)
    returned = lax.all_to_all(gated, "ctx", split_axis=0, concat_axis=1, tiled=True)
    updated = (latent[0].astype(jnp.float32) + returned.astype(jnp.float32)).astype(jnp.bfloat16)
    advanced = passed_along(updated, "step", 1)
    return advanced[None]


def solution(mesh):
    placed = (
        P("step", "ctx", None),
        P("step", "ctx", None),
        P("step", "ctx", None),
        P("step", "ctx", None),
        P(None, "ctx"),
        P(None, "ctx"),
        P(None, "ctx"),
        P(),
        P(),
        P(),
    )
    return jax.shard_map(
        body, mesh=mesh, in_specs=placed, out_specs=P("step", "ctx", None), check_vma=False
    )
```

profile of v0, /device:TPU:1, one launch (start us, length us, event | category | flops | bytes accessed | tf_op | source)
XLA Modules:
  0.0 331.0 jit_solution(3389218791812744334)
XLA Ops:
  6.6 2.8 reshape.192
  9.3 3.6 %reshape.193 = f32[64,32,2,64]{3,2,1,0:T(2,128)} reshape(bf16[1,64,4096]{2,1,0:T(8,128)(2,1)} %param.14) | data formatting | bytes 1572864 | tf_op jit(solution)/shard_map/convert_element_type | solution.py:30
  13.0 0.6 select_reduce_fusion.1
  14.3 0.2 multiply_cosine_fusion
  14.5 7.0 %fusion.57 = (f32[64,32,1,64]{3,2,1,0:T(1,128)S(1)}, f32[64,32,1,64]{3,2,1,0:T(1,128)S(1)}, f32[64,32,1,64]{3,2,1,0:T(1,128)S(1)}, f32[64,32,1,64]{3,2,1,0:T(1,128)S(1)}) fusion(f32[64,32,2,64]{3,2,1,0:T(2,128)} %reshape.193, f32[64,32,2,64]{3,2,1,0:T(2,128)S(1)} %reshape.192), kind=kLoop, calls=%fused_computation.64 | loop fusion | bytes 4194304 | tf_op jit(solution)/shard_map/slice | solution.py:31
  21.4 5.2 %subtract_convert_fusion = (bf16[64,32,1,64]{3,2,0,1:T(2,128)(2,1)S(1)}, bf16[64,32,1,64]{3,2,0,1:T(2,128)(2,1)S(1)}, bf16[64,32,1,64]{3,2,0,1:T(2,128)(2,1)S(1)}, bf16[64,32,1,64]{3,2,0,1:T(2,128)(2,1)}) fusion(f32[64,32,1,64]{3,2,1,0:T(1,128)S(1)} %get-tuple-element.112, f32[64,32,1,64]{3,2,1,0:T(1,128)S(1)} %get-tuple-element.111, ...), kind=kLoop, calls=%fused_computation.43 | loop fusion | flops 2097152 | bytes 3178496 | tf_op jit(solution)/shard_map/convert.5
  26.6 2.8 pad_maximum_fusion.1
  29.4 1.3 convert_element_type.75
  30.7 12.6 %all-to-all-start.1 = ((bf16[64,32,128]{2,0,1:T(8,128)(2,1)}), bf16[64,32,128]{2,0,1:T(8,128)(2,1)S(1)}, u32[]{:S(2)}, u32[]{:S(2)}) async-start(bf16[64,32,128]{2,0,1:T(8,128)(2,1)} %convert_element_type.75), calls=%async_computation.1 | async-start | bytes 1048576 | tf_op jit(solution)/shard_map/all_to_all | solution.py:79
  43.3 0.0 copy-done.3
  43.3 0.1 copy.40
  43.4 1.0 copy.32
  44.4 17.0 %all-to-all-done.1 = bf16[64,32,128]{2,0,1:T(8,128)(2,1)S(1)} async-done(((bf16[64,32,128]{2,0,1:T(8,128)(2,1)}), bf16[64,32,128]{2,0,1:T(8,128)(2,1)S(1)}, u32[]{:S(2)}, u32[]{:S(2)}) %all-to-all-start.1) | async-done | bytes 524320 | tf_op jit(solution)/shard_map/all_to_all | solution.py:79
  61.3 5.7 %all-to-all-start.2 = ((bf16[64,32,128]{2,0,1:T(8,128)(2,1)}), bf16[64,32,128]{2,0,1:T(8,128)(2,1)S(1)}, u32[]{:S(2)}, u32[]{:S(2)}) async-start(bf16[64,32,128]{2,0,1:T(8,128)(2,1)} %copy.32), calls=%async_computation.2 | async-start | bytes 1048576 | tf_op jit(solution)/shard_map/all_to_all | solution.py:80
  67.0 0.2 all-reduce.3.cloned.1.call-start
  67.2 0.9 broadcast_select_fusion.1
  68.1 17.1 %all-to-all-done.2 = bf16[64,32,128]{2,0,1:T(8,128)(2,1)S(1)} async-done(((bf16[64,32,128]{2,0,1:T(8,128)(2,1)}), bf16[64,32,128]{2,0,1:T(8,128)(2,1)S(1)}, u32[]{:S(2)}, u32[]{:S(2)}) %all-to-all-start.2) | async-done | bytes 524320 | tf_op jit(solution)/shard_map/all_to_all | solution.py:80
  85.2 0.9 broadcast_select_fusion
  86.1 0.0 all-reduce.3.cloned.1.call-update
  86.1 3.8 %pad_maximum_fusion = bf16[64,32,2,64]{3,2,0,1:T(2,128)(2,1)S(1)} fusion(bf16[64,32,1,64]{3,2,0,1:T(2,128)(2,1)S(1)} %get-tuple-element.115, bf16[64,32,1,64]{3,2,0,1:T(2,128)(2,1)} %get-tuple-element.116), kind=kLoop, calls=%fused_computation.39 | loop fusion | flops 1048576 | bytes 1048576 | tf_op jit(solution)/shard_map/stack | solution.py:33
  90.0 1.3 convert_element_type.72
  91.3 6.3 %all-to-all-start = ((bf16[64,32,128]{2,0,1:T(8,128)(2,1)}), bf16[64,32,128]{2,0,1:T(8,128)(2,1)}, u32[]{:S(2)}, u32[]{:S(2)}) async-start(bf16[64,32,128]{2,0,1:T(8,128)(2,1)} %convert_element_type.72), calls=%async_computation | async-start | bytes 1048576 | tf_op jit(solution)/shard_map/all_to_all | solution.py:78
  97.6 0.7 select_reduce_fusion
  98.9 0.7 select_reduce_fusion.2
  100.3 0.1 fusion.55
  100.4 0.1 convolution_bitcast_fusion
  100.5 61.0 %all-reduce.3.cloned.1.call-done = (bf16[2048,128]{1,0:T(8,128)(2,1)}, bf16[2048,128]{1,0:T(8,128)(2,1)}) async-done(((bf16[2048,128]{1,0:T(8,128)(2,1)}, bf16[2048,128]{1,0:T(8,128)(2,1)}), (bf16[2048,128]{1,0:T(8,128)(2,1)}, bf16[2048,128]{1,0:T(8,128)(2,1)})) %all-reduce.3.cloned.1.call-update) | async-done | bytes 1048592 | tf_op jit(solution)/shard_map/psum | solution.py:15
  161.5 1.6 maximum_bitcast_fusion
  163.1 2.7 maximum_bitcast_fusion.1
  165.8 0.0 all-to-all-done
  165.8 110.9 %while.11 = (s32[]{:T(128)}, bf16[4,512,128]{2,1,0:T(8,128)(2,1)}, bf16[4,512,1,128]{3,1,2,0:T(8,128)(2,1)}, bf16[8192,1,128]{2,0,1:T(8,128)(2,1)S(1)}, bf16[819...) while((s32[]{:T(128)}, bf16[4,512,128]{2,1,0:T(8,128)(2,1)}, ...), condition=%wide.region_8.9_spmd.clone, body=%wide.region_5.8_spmd.clone.sunk | while | flops 2193923072 | bytes 63221372 | solution.py:123
  165.8 8.0 %fusion.70 = (f32[512]{0:T(512)S(1)}, f32[512,8192]{1,0:T(8,128)}) fusion(pred[8192]{0:T(1024)(128)(4,1)S(1)} %fusion.69, bf16[8192,1,128]{2,0,1:T(8,128)(2,1)S(1)} %get-tuple-element.197, bf16[4,512,1,128]{3,1,2,0:T(8,128)(2,1)} %get-tuple-element.196, s32[]{:T(128)} %get-tuple-element.185), kind=kOutput, calls=%fused_computation.3.clone.1 | convolution fusion | flops 1086324224 | bytes 19016192 | tf_op jit(solution)/shard_map/while/body/eval_jaxpr/qhd,khd->hqk/dot_general | solution.py:107
  173.8 9.9 %fusion.71 = f32[512]{0:T(512)S(1)} fusion(f32[512,8192]{1,0:T(8,128)} %get-tuple-element.174, f32[512]{0:T(512)S(1)} %get-tuple-element.175, pred[8192]{0:T(1024)(128)(4,1)S(1)} %fusion.69), kind=kLoop, calls=%fused_computation.4.clone.1 | loop fusion | flops 16776704 | bytes 16789504 | tf_op jit(solution)/shard_map/while/body/eval_jaxpr/reduce_sum | solution.py:113
  183.8 9.8 %fusion.72 = bf16[4,512,128]{2,1,0:T(8,128)(2,1)} fusion(bf16[4,512,128]{2,1,0:T(8,128)(2,1)} %get-tuple-element.186, s32[]{:T(128)} %get-tuple-element.185, bf16[8192,1,128]{2,0,1:T(8,128)(2,1)S(1)} %copy-done.1, f32[512,8192]{1,0:T(8,128)} %get-tuple-element.174, f32[512]{0:T(512)S(1)} %get-tuple-element.175, pred[8192]{0:T(1024)(128)(4,1)S(1)} %fusion.69, ...), kind=kOutput, calls=%fused_computation.16.clone.1 | convolution fusion | flops 1090715648 | bytes 19018752 | tf_op jit(solution)/shard_map/while/body/eval_jaxpr/hqk,khd->qhd/dot_general | solution.py:114
  193.5 8.0 %fusion.70 = (f32[512]{0:T(512)S(1)}, f32[512,8192]{1,0:T(8,128)}) fusion(pred[8192]{0:T(1024)(128)(4,1)S(1)} %fusion.69, bf16[8192,1,128]{2,0,1:T(8,128)(2,1)S(1)} %get-tuple-element.197, bf16[4,512,1,128]{3,1,2,0:T(8,128)(2,1)} %get-tuple-element.196, s32[]{:T(128)} %get-tuple-element.185), kind=kOutput, calls=%fused_computation.3.clone.1 | convolution fusion | flops 1086324224 | bytes 19016192 | tf_op jit(solution)/shard_map/while/body/eval_jaxpr/qhd,khd->hqk/dot_general | solution.py:107
  201.5 9.9 %fusion.71 = f32[512]{0:T(512)S(1)} fusion(f32[512,8192]{1,0:T(8,128)} %get-tuple-element.174, f32[512]{0:T(512)S(1)} %get-tuple-element.175, pred[8192]{0:T(1024)(128)(4,1)S(1)} %fusion.69), kind=kLoop, calls=%fused_computation.4.clone.1 | loop fusion | flops 16776704 | bytes 16789504 | tf_op jit(solution)/shard_map/while/body/eval_jaxpr/reduce_sum | solution.py:113
  211.5 9.8 %fusion.72 = bf16[4,512,128]{2,1,0:T(8,128)(2,1)} fusion(bf16[4,512,128]{2,1,0:T(8,128)(2,1)} %get-tuple-element.186, s32[]{:T(128)} %get-tuple-element.185, bf16[8192,1,128]{2,0,1:T(8,128)(2,1)S(1)} %copy-done.1, f32[512,8192]{1,0:T(8,128)} %get-tuple-element.174, f32[512]{0:T(512)S(1)} %get-tuple-element.175, pred[8192]{0:T(1024)(128)(4,1)S(1)} %fusion.69, ...), kind=kOutput, calls=%fused_computation.16.clone.1 | convolution fusion | flops 1090715648 | bytes 19018752 | tf_op jit(solution)/shard_map/while/body/eval_jaxpr/hqk,khd->qhd/dot_general | solution.py:114
  221.2 8.0 %fusion.70 = (f32[512]{0:T(512)S(1)}, f32[512,8192]{1,0:T(8,128)}) fusion(pred[8192]{0:T(1024)(128)(4,1)S(1)} %fusion.69, bf16[8192,1,128]{2,0,1:T(8,128)(2,1)S(1)} %get-tuple-element.197, bf16[4,512,1,128]{3,1,2,0:T(8,128)(2,1)} %get-tuple-element.196, s32[]{:T(128)} %get-tuple-element.185), kind=kOutput, calls=%fused_computation.3.clone.1 | convolution fusion | flops 1086324224 | bytes 19016192 | tf_op jit(solution)/shard_map/while/body/eval_jaxpr/qhd,khd->hqk/dot_general | solution.py:107
  229.2 9.9 %fusion.71 = f32[512]{0:T(512)S(1)} fusion(f32[512,8192]{1,0:T(8,128)} %get-tuple-element.174, f32[512]{0:T(512)S(1)} %get-tuple-element.175, pred[8192]{0:T(1024)(128)(4,1)S(1)} %fusion.69), kind=kLoop, calls=%fused_computation.4.clone.1 | loop fusion | flops 16776704 | bytes 16789504 | tf_op jit(solution)/shard_map/while/body/eval_jaxpr/reduce_sum | solution.py:113
  239.2 9.8 %fusion.72 = bf16[4,512,128]{2,1,0:T(8,128)(2,1)} fusion(bf16[4,512,128]{2,1,0:T(8,128)(2,1)} %get-tuple-element.186, s32[]{:T(128)} %get-tuple-element.185, bf16[8192,1,128]{2,0,1:T(8,128)(2,1)S(1)} %copy-done.1, f32[512,8192]{1,0:T(8,128)} %get-tuple-element.174, f32[512]{0:T(512)S(1)} %get-tuple-element.175, pred[8192]{0:T(1024)(128)(4,1)S(1)} %fusion.69, ...), kind=kOutput, calls=%fused_computation.16.clone.1 | convolution fusion | flops 1090715648 | bytes 19018752 | tf_op jit(solution)/shard_map/while/body/eval_jaxpr/hqk,khd->qhd/dot_general | solution.py:114
  248.9 8.0 %fusion.70 = (f32[512]{0:T(512)S(1)}, f32[512,8192]{1,0:T(8,128)}) fusion(pred[8192]{0:T(1024)(128)(4,1)S(1)} %fusion.69, bf16[8192,1,128]{2,0,1:T(8,128)(2,1)S(1)} %get-tuple-element.197, bf16[4,512,1,128]{3,1,2,0:T(8,128)(2,1)} %get-tuple-element.196, s32[]{:T(128)} %get-tuple-element.185), kind=kOutput, calls=%fused_computation.3.clone.1 | convolution fusion | flops 1086324224 | bytes 19016192 | tf_op jit(solution)/shard_map/while/body/eval_jaxpr/qhd,khd->hqk/dot_general | solution.py:107
  256.9 9.9 %fusion.71 = f32[512]{0:T(512)S(1)} fusion(f32[512,8192]{1,0:T(8,128)} %get-tuple-element.174, f32[512]{0:T(512)S(1)} %get-tuple-element.175, pred[8192]{0:T(1024)(128)(4,1)S(1)} %fusion.69), kind=kLoop, calls=%fused_computation.4.clone.1 | loop fusion | flops 16776704 | bytes 16789504 | tf_op jit(solution)/shard_map/while/body/eval_jaxpr/reduce_sum | solution.py:113
  266.9 9.8 %fusion.72 = bf16[4,512,128]{2,1,0:T(8,128)(2,1)} fusion(bf16[4,512,128]{2,1,0:T(8,128)(2,1)} %get-tuple-element.186, s32[]{:T(128)} %get-tuple-element.185, bf16[8192,1,128]{2,0,1:T(8,128)(2,1)S(1)} %copy-done.1, f32[512,8192]{1,0:T(8,128)} %get-tuple-element.174, f32[512]{0:T(512)S(1)} %get-tuple-element.175, pred[8192]{0:T(1024)(128)(4,1)S(1)} %fusion.69, ...), kind=kOutput, calls=%fused_computation.16.clone.1 | convolution fusion | flops 1090715648 | bytes 19018752 | tf_op jit(solution)/shard_map/while/body/eval_jaxpr/hqk,khd->qhd/dot_general | solution.py:114
  276.6 33.1 %all_to_all.61 = bf16[32,64,128]{2,1,0:T(8,128)(2,1)S(1)} all-to-all(bf16[32,64,128]{2,1,0:T(8,128)(2,1)} %bitcast.105), channel_id=1, replica_groups=mesh['step'=8,'ctx'=32] {'ctx'}, dimensions={0} | all-to-all | bytes 1048576 | tf_op jit(solution)/shard_map/all_to_all | solution.py:124
  309.7 0.1 fusion.54
  309.8 0.1 collective-permute-start
  309.9 13.4 %collective-permute-done = bf16[64,4096]{1,0:T(8,128)(2,1)S(1)} collective-permute-done((bf16[64,4096]{1,0:T(8,128)(2,1)S(1)}, bf16[64,4096]{1,0:T(8,128)(2,1)S(1)}, u32[]{:S(2)}, u32[]{:S(2)}) %collective-permute-start) | collective-permute-done | bytes 524320 | tf_op jit(solution)/shard_map/ppermute | solution.py:21
  323.3 0.8 copy.62
  (29 shorter events, 0.1 us)
Async XLA Ops:
  6.5 93.8 %copy-start = (bf16[256,128]{1,0:T(8,128)(2,1)S(1)}, bf16[256,128]{1,0:T(8,128)(2,1)}, u32[]{:S(2)}) copy-start(bf16[256,128]{1,0:T(8,128)(2,1)} %param.18) | copy-start | bytes 196612
  6.5 6.4 %copy-start.5 = (s32[8]{0:T(128)S(1)}, s32[8]{0:T(128)}, u32[]{:S(2)}) copy-start(s32[8]{0:T(128)} %param.20) | copy-start | bytes 100
  26.6 16.7 %copy-start.3 = (bf16[1,64,4096]{2,1,0:T(8,128)(2,1)S(1)}, bf16[1,64,4096]{2,1,0:T(8,128)(2,1)}, u32[]{:S(2)}) copy-start(bf16[1,64,4096]{2,1,0:T(8,128)(2,1)} %param.15) | copy-start | bytes 1572868
  30.7 30.7 %all-to-all-start.1 = ((bf16[64,32,128]{2,0,1:T(8,128)(2,1)}), bf16[64,32,128]{2,0,1:T(8,128)(2,1)S(1)}, u32[]{:S(2)}, u32[]{:S(2)}) async-start(bf16[64,32,128]{2,0,1:T(8,128)(2,1)} %convert_element_type.75), calls=%async_computation.1 | async-start | bytes 1048576 | tf_op jit(solution)/shard_map/all_to_all | solution.py:79
  61.3 23.9 %all-to-all-start.2 = ((bf16[64,32,128]{2,0,1:T(8,128)(2,1)}), bf16[64,32,128]{2,0,1:T(8,128)(2,1)S(1)}, u32[]{:S(2)}, u32[]{:S(2)}) async-start(bf16[64,32,128]{2,0,1:T(8,128)(2,1)} %copy.32), calls=%async_computation.2 | async-start | bytes 1048576 | tf_op jit(solution)/shard_map/all_to_all | solution.py:80
  67.0 94.5 %all-reduce.3.cloned.1.call-start = ((), (), s32[]{:S(2)}) async-start(), calls=%async_computation.4 | async-start | bytes 2097152 | tf_op jit(solution)/shard_map/psum | solution.py:15
  68.1 29.4 %copy-start.6 = (s32[8]{0:T(128)S(1)}, s32[8]{0:T(128)}, u32[]{:S(2)}) copy-start(s32[8]{0:T(128)} %param.19) | copy-start | bytes 100
  68.1 30.8 %copy-start.7 = (s32[8]{0:T(128)S(1)}, s32[8]{0:T(128)}, u32[]{:S(2)}) copy-start(s32[8]{0:T(128)} %param.21) | copy-start | bytes 100
  91.3 74.5 %all-to-all-start = ((bf16[64,32,128]{2,0,1:T(8,128)(2,1)}), bf16[64,32,128]{2,0,1:T(8,128)(2,1)}, u32[]{:S(2)}, u32[]{:S(2)}) async-start(bf16[64,32,128]{2,0,1:T(8,128)(2,1)} %convert_element_type.72), calls=%async_computation | async-start | bytes 1048576 | tf_op jit(solution)/shard_map/all_to_all | solution.py:78
  161.5 1.6 copy-start.4
  165.8 143.9 %copy-start.2 = (bf16[1,64,4096]{2,1,0:T(8,128)(2,1)S(1)}, bf16[1,64,4096]{2,1,0:T(8,128)(2,1)}, u32[]{:S(2)}) copy-start(bf16[1,64,4096]{2,1,0:T(8,128)(2,1)} %param.12) | copy-start | bytes 1572868
  173.8 9.9 %copy-start.1 = (bf16[8192,1,128]{2,0,1:T(8,128)(2,1)S(1)}, bf16[8192,1,128]{2,0,1:T(8,128)(2,1)}, u32[]{:S(2)}) copy-start(bf16[8192,1,128]{2,0,1:T(8,128)(2,1)} %get-tuple-element.198) | copy-start | bytes 6291460 | tf_op jit(solution)/shard_map/while
  201.5 9.9 %copy-start.1 = (bf16[8192,1,128]{2,0,1:T(8,128)(2,1)S(1)}, bf16[8192,1,128]{2,0,1:T(8,128)(2,1)}, u32[]{:S(2)}) copy-start(bf16[8192,1,128]{2,0,1:T(8,128)(2,1)} %get-tuple-element.198) | copy-start | bytes 6291460 | tf_op jit(solution)/shard_map/while
  229.2 9.9 %copy-start.1 = (bf16[8192,1,128]{2,0,1:T(8,128)(2,1)S(1)}, bf16[8192,1,128]{2,0,1:T(8,128)(2,1)}, u32[]{:S(2)}) copy-start(bf16[8192,1,128]{2,0,1:T(8,128)(2,1)} %get-tuple-element.198) | copy-start | bytes 6291460 | tf_op jit(solution)/shard_map/while
  256.9 9.9 %copy-start.1 = (bf16[8192,1,128]{2,0,1:T(8,128)(2,1)S(1)}, bf16[8192,1,128]{2,0,1:T(8,128)(2,1)}, u32[]{:S(2)}) copy-start(bf16[8192,1,128]{2,0,1:T(8,128)(2,1)} %get-tuple-element.198) | copy-start | bytes 6291460 | tf_op jit(solution)/shard_map/while
  309.8 13.5 %collective-permute-start = (bf16[64,4096]{1,0:T(8,128)(2,1)S(1)}, bf16[64,4096]{1,0:T(8,128)(2,1)S(1)}, u32[]{:S(2)}, u32[]{:S(2)}) collective-permute-start(bf16[64,4096]{1,0:T(8,128)(2,1)S(1)} %fusion.54), channel_id=1, source_target_pairs={{224,0},{0,32},{32,64},{64,96},{96,128},{128,160},{160,192},{192,2... | collective-permute-start | bytes 1572872 | tf_op jit(solution)/shard_map/ppermute | solution.py:21
Sparse Core Ops, SparseCore 0:
  86.2 75.1 all-reduce.2
where the time goes:
time: 333 us; the launch traced here: 331 us
  waiting for transfers between devices  108 us (32%)
  matrix products  71.2 us (21%)
  other arithmetic  60 us (18%)
  blocking collectives  33.1 us (10%)
  starting transfers between devices  24.8 us (7%)
  local copies, waits for them, and re-layouts  17.8 us (5%)
  between operations  15.6 us (5%)
    psum x1, waiting for transfers between devices, from_root(): return lax.psum(jnp.where(mine, shard, jnp.zeros_like(shard)), axis)  61 us
    reduce_sum x4, other arithmetic, attend_block(): totals = jnp.sum(weights, axis=2)  39.8 us
    dot_general x4, matrix products, attend_block(): jnp.einsum('hqk,khd->qhd', weights.astype(jnp.bfloat16), values_all, pref...  39.1 us
    all_to_all x1, blocking collectives, body(): lax.all_to_all(gated, 'ctx', split_axis=0, concat_axis=1, tiled=True)  33.1 us
    dot_general x4, matrix products, attend_block(): jnp.einsum('qhd,khd->hqk', query_block, keys_all, preferred_element_type=...  32 us
    all_to_all x1, waiting for transfers between devices, body(): lax.all_to_all(own_values, 'ctx', split_axis=1, concat_axis=0, tiled=True)  17.1 us
    all_to_all x1, waiting for transfers between devices, body(): lax.all_to_all(own_keys, 'ctx', split_axis=1, concat_axis=0, tiled=True)  17 us
    ppermute x1, waiting for transfers between devices, passed_along(): return lax.ppermute(block, axis, route)  13.4 us
  transfers between devices with their start and end apart: 5, of which 4 were waited for; matrix products, arithmetic and copies ran while one was open for 4% of the time, Pallas kernels for 0%

commit v1 on v0

v1 whole, which is shorter than its diff:
```python
import functools
import math

import jax
import jax.numpy as jnp
import numpy as np
from jax import lax
from jax.experimental import pallas as pl
from jax.experimental.pallas import tpu as pltpu
from jax.sharding import PartitionSpec as P

MESH = pl.DeviceIdType.MESH
HEAD_DIM = 128
FREQS = 256
FRAMES = 3
BLOCK = 256
CHUNK = 512
FAR = 1e30

TREES = (
    ((0, 1, 2, 6), (5,), (1, 2)),
    ((7,), (0, 3, 2, 7, 6), (3,)),
    ((4, 5), (4,), (0, 6, 5, 7)),
)
PART_ROWS = (704, 640, 704)
PARTS = 4


def table():
    n = FREQS // 2
    gate = 10000.0 ** (-np.arange(n, dtype=np.float64) / n)
    half = HEAD_DIM // 2
    turn = 10000.0 ** (-np.arange(half, dtype=np.float64) / half)
    rows = np.concatenate([np.repeat(gate[:, None], 128, 1), np.repeat(np.tile(turn, 2)[None], 8, 0)])
    return rows.astype(np.float32)


def kernel(
    times_ref, spans_ref, prefix_ref, freq_ref, latent_ref, q_ref, k_ref, v_ref, ck_ref, cv_ref, tw_ref,
    moved_ref, gated_ref,
    freq, q_in, k_in, ck, cv, tw, q_out, k_out, qh, kh, vh, kc, vc, acc, peak, gate, mine,
    load_sem, q_sent, q_got, kv_sent, kv_got, c_sent, c_got, o_sent, o_got, l_sent, l_got, next_in,
):
    groups, width = lax.axis_size("step"), lax.axis_size("ctx")
    g, me = lax.axis_index("step"), lax.axis_index("ctx")
    rows = q_ref.shape[0]
    total = rows * width
    blocks = total // BLOCK
    per = BLOCK // rows
    last = groups - 1
    clean = g == last
    after, before = lax.rem(g + 1, groups), lax.rem(g + groups - 1, groups)
    gx, gy = lax.div(g, 4), lax.rem(g, 4)
    near = (
        gx * 4 + lax.rem(gy + 1, 4),
        gx * 4 + lax.rem(gy + 3, 4),
        (1 - gx) * 4 + gy,
    )
    node = (1 - gx) * 4 + lax.rem(gy + 1, 4)

    loads = [
        pltpu.make_async_copy(a, b, load_sem.at[i])
        for i, (a, b) in enumerate(
            ((q_ref, q_in), (k_ref, k_in), (freq_ref, freq), (tw_ref, tw), (ck_ref, ck), (cv_ref, cv))
        )
    ]
    for load in loads:
        load.start()

    barrier = pltpu.get_barrier_semaphore()

    def greet(i, _):
        pl.semaphore_signal(barrier, inc=1, device_id={"ctx": lax.rem(me + i, width)}, device_id_type=MESH)
        return 0

    lax.fori_loop(1, width, greet, 0)
    for other in near + (after, before):
        pl.semaphore_signal(barrier, inc=1, device_id={"step": other}, device_id_type=MESH)

    loads[2].wait()
    row = me * rows + lax.broadcasted_iota(jnp.int32, (rows, 128), 0)
    frames = spans_ref[g] * FRAMES + lax.div(row * FRAMES, total)
    angles = frames.astype(jnp.float32) * freq[128:129, :]
    cosine = jnp.cos(angles)
    lane = lax.broadcasted_iota(jnp.int32, (rows, 128), 1)
    sine = jnp.where(lane < HEAD_DIM // 2, -jnp.sin(angles), jnp.sin(angles))
    scale = math.log2(math.e) / math.sqrt(HEAD_DIM)
    loads[0].wait()
    loads[1].wait()

    def turn(h, _):
        cols = pl.ds(pl.multiple_of(h * 128, 128), 128)
        q = q_in[:, cols].astype(jnp.float32)
        k = k_in[:, cols].astype(jnp.float32)
        q_out[h] = ((q * cosine + pltpu.roll(q, 64, 1) * sine) * scale).astype(jnp.bfloat16)
        k_out[h] = (k * cosine + pltpu.roll(k, 64, 1) * sine).astype(jnp.bfloat16)
        return 0

    lax.fori_loop(0, width, turn, 0)
    pl.semaphore_wait(barrier, width - 1 + 5)
    pl.semaphore_signal(next_in, inc=1, device_id={"step": before}, device_id_type=MESH)

    my_rows = pl.ds(pl.multiple_of(me * rows, rows), rows)
    my_block = lax.div(me, per)

    def q_to(t):
        return pltpu.make_async_remote_copy(
            q_out.at[t], qh.at[my_rows], q_sent, q_got.at[my_block], device_id={"ctx": t}, device_id_type=MESH
        )

    def k_to(t):
        return pltpu.make_async_remote_copy(
            k_out.at[t], kh.at[my_rows], kv_sent.at[0], kv_got.at[0], device_id={"ctx": t}, device_id_type=MESH
        )

    def v_of(t):
        return v_ref.at[:, pl.ds(pl.multiple_of(t * 128, 128), 128)]

    def v_to(t):
        return pltpu.make_async_remote_copy(
            v_of(t), vh.at[my_rows], kv_sent.at[1], kv_got.at[1], device_id={"ctx": t}, device_id_type=MESH
        )

    def send_all(copy_to):
        def send(i, _):
            copy_to(lax.rem(me + i, width)).start()
            return 0

        lax.fori_loop(1, width, send, 0)

    @pl.when(jnp.logical_not(clean))
    def _():
        send_all(q_to)

    send_all(k_to)
    send_all(v_to)

    @pl.when(clean)
    def _():
        send_all(q_to)

    pltpu.make_async_copy(q_out.at[me], qh.at[my_rows], q_got.at[my_block]).start()
    pltpu.make_async_copy(k_out.at[me], kh.at[my_rows], kv_got.at[0]).start()
    pltpu.make_async_copy(v_of(me), vh.at[my_rows], kv_got.at[1]).start()
    latent_copy = pltpu.make_async_remote_copy(
        latent_ref, moved_ref, l_sent, l_got, device_id={"step": after}, device_id_type=MESH
    )
    latent_copy.start()

    loads[3].wait()
    turns = times_ref[g].astype(jnp.float32) * freq[0:128, :]
    gate[...] = jnp.sum(
        jnp.cos(turns) * tw[0:128, :].astype(jnp.float32) + jnp.sin(turns) * tw[128:256, :].astype(jnp.float32),
        axis=0,
        keepdims=True,
    )
    loads[4].wait()
    loads[5].wait()

    def passes(tree, way):
        return functools.reduce(jnp.logical_or, [node == n for n in TREES[tree][way]])

    def part_rows(tree, part):
        size = PART_ROWS[tree] // PARTS
        return pl.ds(sum(PART_ROWS[:tree]) + part * size, size)

    def part_copy(source, target, which, tree, part, way):
        return pltpu.make_async_remote_copy(
            source.at[part_rows(tree, part)],
            target.at[part_rows(tree, part)],
            c_sent.at[which, tree, way],
            c_got.at[which, tree, part],
            device_id={"step": near[way]},
            device_id_type=MESH,
        )

    def start_clean(source, target, which):
        for part in range(PARTS):
            for tree in range(3):
                for way in range(3):
                    if 0 in TREES[tree][way]:
                        part_copy(source, target, which, tree, part, way).start()

    def pass_clean(target, which):
        for part in range(PARTS):
            for tree in range(3):
                place = target.at[part_rows(tree, part)]
                pltpu.make_async_copy(place, place, c_got.at[which, tree, part]).wait()
                for way in range(3):
                    if any(n != 0 for n in TREES[tree][way]):

                        @pl.when(passes(tree, way))
                        def _():
                            part_copy(target, target, which, tree, part, way).start()

    def got(place, sem):
        pltpu.make_async_copy(place, place, sem).wait()

    far = (2 - prefix_ref[g]).astype(jnp.float32) * FAR
    ones = jnp.ones((CHUNK, 128), jnp.bfloat16)

    def attend(state, q, keys, values, start, stop, masked):
        for at in range(start, stop, CHUNK):
            s = lax.dot_general(
                q, keys[at : at + CHUNK, :], (((1,), (1,)), ((), ())), preferred_element_type=jnp.float32
            )
            top = jnp.max(s, axis=1, keepdims=True)
            if masked:
                top = top - far
            if state is not None:
                old, total_so_far = state
                top = jnp.maximum(old, top)
            p = jnp.exp2(s - (top + far if masked else top)).astype(jnp.bfloat16)
            mixed = jnp.dot(
                p, jnp.concatenate([values[at : at + CHUNK, :], ones], axis=1), preferred_element_type=jnp.float32
            )
            if state is not None:
                mixed = mixed + total_so_far * jnp.exp2(old - top)
            state = top, mixed
        return state

    def step(i, _):
        first = jnp.where(clean, lax.rem(i, 2) == 0, i < blocks)
        count = jnp.where(clean, lax.div(i, 2), lax.rem(i, blocks))
        block = lax.rem(my_block + 2 * blocks - 1 - count, blocks)
        here = pl.ds(pl.multiple_of(block * BLOCK, BLOCK), BLOCK)

        @pl.when(jnp.logical_and(jnp.logical_not(clean), i == blocks // 2))
        def _():
            pass_clean(kc, 0)

        @pl.when(jnp.logical_and(jnp.logical_not(clean), i == blocks))
        def _():
            pass_clean(vc, 1)
            got(kh, kv_got.at[0])
            got(vh, kv_got.at[1])

        @pl.when(i == jnp.where(clean, 1, blocks))
        def _():
            pl.semaphore_wait(next_in, 1)

        @pl.when(first)
        def _():
            got(qh.at[here], q_got.at[block])
            q = qh[here, :]
            state = attend(None, q, ck, cv, total, 2 * total, False)
            top, mixed = attend(state, q, ck, cv, 0, total, True)
            acc[here, :] = mixed
            peak[here, :] = jnp.broadcast_to(top, (BLOCK, 128))

        @pl.when(jnp.logical_not(first))
        def _():
            q = qh[here, :]

            @pl.when(jnp.logical_not(clean))
            def _():
                top, mixed = attend((peak[here, 0:1], acc[here, :]), q, kc, vc, 0, total, False)
                acc[here, :] = mixed
                peak[here, :] = jnp.broadcast_to(top, (BLOCK, 128))

            _, mixed = attend((peak[here, 0:1], acc[here, :]), q, kh, vh, 0, total, False)
            mine[here, :] = (mixed[:, :128] / mixed[:, 128:] * gate[...]).astype(jnp.bfloat16)
            for s in range(per):
                owner = block * per + s
                pltpu.make_async_remote_copy(
                    mine.at[pl.ds(pl.multiple_of(owner * rows, rows), rows)],
                    gated_ref.at[:, pl.ds(pl.multiple_of(me * 128, 128), 128)],
                    o_sent,
                    o_got,
                    device_id={"step": after, "ctx": owner},
                    device_id_type=MESH,
                ).start()

        return 0

    @pl.when(clean)
    def _():
        got(kh, kv_got.at[0])
        start_clean(kh, kc, 0)
        got(vh, kv_got.at[1])
        start_clean(vh, vc, 1)

    lax.fori_loop(0, 2 * blocks, step, 0)

    sent = qh.at[pl.ds(0, total - rows)]
    got(sent, q_sent)
    got(sent, kv_sent.at[0])
    got(sent, kv_sent.at[1])
    for which in range(2):
        for tree in range(3):
            place = kc.at[pl.ds(0, PART_ROWS[tree])]
            for way in range(3):

                @pl.when(passes(tree, way))
                def _():
                    got(place, c_sent.at[which, tree, way])

    latent_copy.wait()
    got(mine, o_sent)
    got(gated_ref, o_got)


def body(latent, q, k, v, cache_keys, cache_values, time_weight, timestep, span_index, prefix_spans):
    rows, width = q.shape[1:]
    total = cache_keys.shape[0] // 2
    half = jnp.bfloat16
    smem = pl.BlockSpec(memory_space=pltpu.SMEM)
    hbm = pl.BlockSpec(memory_space=pl.ANY)
    dma = pltpu.SemaphoreType.DMA
    freqs = table()
    moved, gated = pl.pallas_call(
        kernel,
        out_shape=[jax.ShapeDtypeStruct((rows, width), half)] * 2,
        in_specs=[smem] * 3 + [hbm] * 8,
        out_specs=[hbm] * 2,
        scratch_shapes=[
            pltpu.VMEM(freqs.shape, jnp.float32),
            pltpu.VMEM((rows, width), half),
            pltpu.VMEM((rows, width), half),
            pltpu.VMEM((2 * total, 128), half),
            pltpu.VMEM((2 * total, 128), half),
            pltpu.VMEM((FREQS, 128), half),
            pltpu.VMEM((width // 128, rows, 128), half),
            pltpu.VMEM((width // 128, rows, 128), half),
            pltpu.VMEM((total, 128), half),
            pltpu.VMEM((total, 128), half),
            pltpu.VMEM((total, 128), half),
            pltpu.VMEM((total, 128), half),
            pltpu.VMEM((total, 128), half),
            pltpu.VMEM((total, 256), jnp.float32),
            pltpu.VMEM((total, 128), jnp.float32),
            pltpu.VMEM((1, 128), jnp.float32),
            pltpu.VMEM((total, 128), half),
            dma((6,)),
            dma,
            dma((total // BLOCK,)),
            dma((2,)),
            dma((2,)),
            dma((2, 3, 3)),
            dma((2, 3, PARTS)),
            dma,
            dma,
            dma,
            dma,
            pltpu.SemaphoreType.REGULAR,
        ],
        compiler_params=pltpu.CompilerParams(
            collective_id=0, has_side_effects=True, vmem_limit_bytes=56 * 1024 * 1024
        ),
    )(timestep, span_index, prefix_spans, jnp.asarray(freqs), latent[0], q[0], k[0], v[0], cache_keys, cache_values, time_weight)
    advanced = (moved.astype(jnp.float32) + gated.astype(jnp.float32)).astype(half)
    return advanced[None]


def solution(mesh):
    spans = P("step", "ctx", None)
    heads = P(None, "ctx")
    return jax.shard_map(
        body,
        mesh=mesh,
        in_specs=(spans,) * 4 + (heads,) * 3 + (P(),) * 3,
        out_specs=spans,
        check_vma=False,
    )
```

time: 333 us -> 226 us (0.68)
  the two profiles are of different devices: /device:TPU:1 before, /device:TPU:23 now
where the time goes in v1:
time: 226 us
  Pallas kernels  223 us (99%)
    pallas_call x1, Pallas kernels, body(): pl.pallas_call(kernel, out_shape=[jax.ShapeDtypeStruct((rows, width), hal...  223 us

profile of v1, /device:TPU:23, one launch (start us, length us, event | category | flops | bytes accessed | tf_op | source)
XLA Modules:
  0.0 225.6 jit_solution(5226972213435713947)
XLA Ops:
  0.0 223.5 %shard_map.109 = (bf16[64,4096]{1,0:T(8,128)(2,1)}, bf16[64,4096]{1,0:T(8,128)(2,1)}) custom-call(s32[8]{0:T(128)} %times_ref.1, s32[8]{0:T(128)} %spans_ref.1, s32[8]{0:T(128)} %prefix_ref.1, f32[136,128]{1,0:T(8,128)} %constant.2.clone.freq_ref, bf16[64,4096]{1,0:T(8,128)(2,1)} %bitcast.6, bf16[64,4096]{1,0:T(8,128)(2,1)} %bitcast.7, ...), custom_call_target="tpu_custom_call" | custom-call | tf_op jit(solution)/shard_map/pallas_call | solution.py:311
  223.5 2.1 fusion

commit v2 on v1

--- a/solution.py
+++ b/solution.py
@@ -17,13 +17,10 @@
 CHUNK = 512
 FAR = 1e30
 
-TREES = (
-    ((0, 1, 2, 6), (5,), (1, 2)),
-    ((7,), (0, 3, 2, 7, 6), (3,)),
-    ((4, 5), (4,), (0, 6, 5, 7)),
-)
-PART_ROWS = (704, 640, 704)
-PARTS = 4
+
+EARLY = 24
+PASS_KEYS = 2
+PASS_VALUES = 8
 
 
 def table():
@@ -39,7 +36,7 @@
     times_ref, spans_ref, prefix_ref, freq_ref, latent_ref, q_ref, k_ref, v_ref, ck_ref, cv_ref, tw_ref,
     moved_ref, gated_ref,
     freq, q_in, k_in, ck, cv, tw, q_out, k_out, qh, kh, vh, kc, vc, acc, peak, gate, mine,
-    load_sem, q_sent, q_got, kv_sent, kv_got, c_sent, c_got, o_sent, o_got, l_sent, l_got, next_in,
+    load_sem, q_sent, k_sent, v_sent, q_got, kv_got, hold_got, first_sent, c_sent, c_got, o_sent, o_got, l_sent, l_got, next_in, all_in,
 ):
     groups, width = lax.axis_size("step"), lax.axis_size("ctx")
     g, me = lax.axis_index("step"), lax.axis_index("ctx")
@@ -50,13 +47,7 @@
     last = groups - 1
     clean = g == last
     after, before = lax.rem(g + 1, groups), lax.rem(g + groups - 1, groups)
-    gx, gy = lax.div(g, 4), lax.rem(g, 4)
-    near = (
-        gx * 4 + lax.rem(gy + 1, 4),
-        gx * 4 + lax.rem(gy + 3, 4),
-        (1 - gx) * 4 + gy,
-    )
-    node = (1 - gx) * 4 + lax.rem(gy + 1, 4)
+    held = lax.rem(g + groups * width - me, groups)
 
     loads = [
         pltpu.make_async_copy(a, b, load_sem.at[i])
@@ -74,8 +65,12 @@
         return 0
 
     lax.fori_loop(1, width, greet, 0)
-    for other in near + (after, before):
-        pl.semaphore_signal(barrier, inc=1, device_id={"step": other}, device_id_type=MESH)
+
+    def greet_step(i, _):
+        pl.semaphore_signal(barrier, inc=1, device_id={"step": lax.rem(g + i, groups)}, device_id_type=MESH)
+        return 0
+
+    lax.fori_loop(1, groups, greet_step, 0)
 
     loads[2].wait()
     row = me * rows + lax.broadcasted_iota(jnp.int32, (rows, 128), 0)
@@ -97,51 +92,113 @@
         return 0
 
     lax.fori_loop(0, width, turn, 0)
-    pl.semaphore_wait(barrier, width - 1 + 5)
+    pl.semaphore_wait(barrier, width + groups - 2)
     pl.semaphore_signal(next_in, inc=1, device_id={"step": before}, device_id_type=MESH)
+
+    @pl.when(jnp.logical_not(clean))
+    def _():
+        pl.semaphore_signal(all_in, inc=1, device_id={"step": last}, device_id_type=MESH)
 
     my_rows = pl.ds(pl.multiple_of(me * rows, rows), rows)
     my_block = lax.div(me, per)
 
-    def q_to(t):
-        return pltpu.make_async_remote_copy(
-            q_out.at[t], qh.at[my_rows], q_sent, q_got.at[my_block], device_id={"ctx": t}, device_id_type=MESH
-        )
-
-    def k_to(t):
-        return pltpu.make_async_remote_copy(
-            k_out.at[t], kh.at[my_rows], kv_sent.at[0], kv_got.at[0], device_id={"ctx": t}, device_id_type=MESH
-        )
-
     def v_of(t):
         return v_ref.at[:, pl.ds(pl.multiple_of(t * 128, 128), 128)]
 
-    def v_to(t):
-        return pltpu.make_async_remote_copy(
-            v_of(t), vh.at[my_rows], kv_sent.at[1], kv_got.at[1], device_id={"ctx": t}, device_id_type=MESH
-        )
-
-    def send_all(copy_to):
+    def got(place, sem):
+        pltpu.make_async_copy(place, place, sem).wait()
+
+    def send_all(source, target, sent, arrived):
         def send(i, _):
-            copy_to(lax.rem(me + i, width)).start()
+            to = lax.rem(me + i, width)
+            pltpu.make_async_remote_copy(
+                source(to),
+                target.at[my_rows],
+                sent.at[jnp.where(i <= EARLY, 0, 1)],
+                arrived,
+                device_id={"ctx": to},
+                device_id_type=MESH,
+            ).start()
             return 0
 
         lax.fori_loop(1, width, send, 0)
+        pltpu.make_async_copy(source(me), target.at[my_rows], arrived).start()
+
+    def send_clean(source, target, sent, which):
+        def copy_to(to, sem):
+            return pltpu.make_async_remote_copy(
+                source(to),
+                target.at[my_rows],
+                sem,
+                hold_got.at[which],
+                device_id={"step": lax.rem(my_block + to, groups), "ctx": to},
+                device_id_type=MESH,
+            )
+
+        def send(i, _):
+            copy_to(lax.rem(me + i, width), sent.at[jnp.where(i <= EARLY, 0, 1)]).start()
+            return 0
+
+        lax.fori_loop(1, width, send, 0)
+
+        @pl.when(own_holder)
+        def _():
+            pltpu.make_async_copy(source(me), target.at[my_rows], hold_got.at[which]).start()
+
+        @pl.when(jnp.logical_not(own_holder))
+        def _():
+            copy_to(me, first_sent.at[which]).start()
+
+    own_holder = lax.rem(my_block + me, groups) == g
+
+    def send_q():
+        send_all(lambda t: q_out.at[t], qh, q_sent, q_got.at[my_block])
+
+    def send_k():
+        send_all(lambda t: k_out.at[t], kh, k_sent, kv_got.at[0])
+
+    def send_v():
+        send_all(v_of, vh, v_sent, kv_got.at[1])
+
+    def hand_on(target, which):
+        part = target.at[pl.ds(pl.multiple_of(held * BLOCK, BLOCK), BLOCK)]
+        got(part, hold_got.at[which])
+
+        def send(i, _):
+            pltpu.make_async_remote_copy(
+                part,
+                part,
+                c_sent.at[which],
+                c_got.at[which],
+                device_id={"step": lax.rem(g + i, groups)},
+                device_id_type=MESH,
+            ).start()
+            return 0
+
+        lax.fori_loop(1, groups, send, 0)
+
+    others = kc.at[pl.ds(0, (groups - 1) * BLOCK)]
+    early = qh.at[pl.ds(0, EARLY * rows)]
+    late = qh.at[pl.ds(0, (width - 1 - EARLY) * rows)]
 
     @pl.when(jnp.logical_not(clean))
     def _():
-        send_all(q_to)
-
-    send_all(k_to)
-    send_all(v_to)
+        send_q()
+        got(early, q_sent.at[0])
+        send_k()
+        send_v()
 
     @pl.when(clean)
     def _():
-        send_all(q_to)
-
-    pltpu.make_async_copy(q_out.at[me], qh.at[my_rows], q_got.at[my_block]).start()
-    pltpu.make_async_copy(k_out.at[me], kh.at[my_rows], kv_got.at[0]).start()
-    pltpu.make_async_copy(v_of(me), vh.at[my_rows], kv_got.at[1]).start()
+        pl.semaphore_wait(all_in, groups - 1)
+        send_clean(lambda t: k_out.at[t], kc, k_sent, 0)
+        got(early, k_sent.at[0])
+        send_clean(v_of, vc, v_sent, 1)
+        hand_on(kc, 0)
+        got(early, v_sent.at[0])
+        send_q()
+        hand_on(vc, 1)
+
     latent_copy = pltpu.make_async_remote_copy(
         latent_ref, moved_ref, l_sent, l_got, device_id={"step": after}, device_id_type=MESH
     )
@@ -156,45 +213,6 @@
     )
     loads[4].wait()
     loads[5].wait()
-
-    def passes(tree, way):
-        return functools.reduce(jnp.logical_or, [node == n for n in TREES[tree][way]])
-
-    def part_rows(tree, part):
-        size = PART_ROWS[tree] // PARTS
-        return pl.ds(sum(PART_ROWS[:tree]) + part * size, size)
-
-    def part_copy(source, target, which, tree, part, way):
-        return pltpu.make_async_remote_copy(
-            source.at[part_rows(tree, part)],
-            target.at[part_rows(tree, part)],
-            c_sent.at[which, tree, way],
-            c_got.at[which, tree, part],
-            device_id={"step": near[way]},
-            device_id_type=MESH,
-        )
-
-    def start_clean(source, target, which):
-        for part in range(PARTS):
-            for tree in range(3):
-                for way in range(3):
-                    if 0 in TREES[tree][way]:
-                        part_copy(source, target, which, tree, part, way).start()
-
-    def pass_clean(target, which):
-        for part in range(PARTS):
-            for tree in range(3):
-                place = target.at[part_rows(tree, part)]
-                pltpu.make_async_copy(place, place, c_got.at[which, tree, part]).wait()
-                for way in range(3):
-                    if any(n != 0 for n in TREES[tree][way]):
-
-                        @pl.when(passes(tree, way))
-                        def _():
-                            part_copy(target, target, which, tree, part, way).start()
-
-    def got(place, sem):
-        pltpu.make_async_copy(place, place, sem).wait()
 
     far = (2 - prefix_ref[g]).astype(jnp.float32) * FAR
     ones = jnp.ones((CHUNK, 128), jnp.bfloat16)
@@ -225,19 +243,24 @@
         block = lax.rem(my_block + 2 * blocks - 1 - count, blocks)
         here = pl.ds(pl.multiple_of(block * BLOCK, BLOCK), BLOCK)
 
-        @pl.when(jnp.logical_and(jnp.logical_not(clean), i == blocks // 2))
-        def _():
-            pass_clean(kc, 0)
+        @pl.when(jnp.logical_and(jnp.logical_not(clean), i == PASS_KEYS))
+        def _():
+            hand_on(kc, 0)
+
+        @pl.when(jnp.logical_and(jnp.logical_not(clean), i == PASS_VALUES))
+        def _():
+            hand_on(vc, 1)
+
+        @pl.when(i == jnp.where(clean, 1, blocks))
+        def _():
+            pl.semaphore_wait(next_in, 1)
+            got(others, c_got.at[0])
+            got(others, c_got.at[1])
 
         @pl.when(jnp.logical_and(jnp.logical_not(clean), i == blocks))
         def _():
-            pass_clean(vc, 1)
             got(kh, kv_got.at[0])
             got(vh, kv_got.at[1])
-
-        @pl.when(i == jnp.where(clean, 1, blocks))
-        def _():
-            pl.semaphore_wait(next_in, 1)
 
         @pl.when(first)
         def _():
@@ -251,14 +274,16 @@
         @pl.when(jnp.logical_not(first))
         def _():
             q = qh[here, :]
+            top, mixed = attend((peak[here, 0:1], acc[here, :]), q, kc, vc, 0, total, False)
+            acc[here, :] = mixed
+            peak[here, :] = jnp.broadcast_to(top, (BLOCK, 128))
 
             @pl.when(jnp.logical_not(clean))
             def _():
-                top, mixed = attend((peak[here, 0:1], acc[here, :]), q, kc, vc, 0, total, False)
+                _, mixed = attend((peak[here, 0:1], acc[here, :]), q, kh, vh, 0, total, False)
                 acc[here, :] = mixed
-                peak[here, :] = jnp.broadcast_to(top, (BLOCK, 128))
-
-            _, mixed = attend((peak[here, 0:1], acc[here, :]), q, kh, vh, 0, total, False)
+
+            mixed = acc[here, :]
             mine[here, :] = (mixed[:, :128] / mixed[:, 128:] * gate[...]).astype(jnp.bfloat16)
             for s in range(per):
                 owner = block * per + s
@@ -273,27 +298,25 @@
 
         return 0
 
+    lax.fori_loop(0, 2 * blocks, step, 0)
+
     @pl.when(clean)
     def _():
-        got(kh, kv_got.at[0])
-        start_clean(kh, kc, 0)
-        got(vh, kv_got.at[1])
-        start_clean(vh, vc, 1)
-
-    lax.fori_loop(0, 2 * blocks, step, 0)
-
-    sent = qh.at[pl.ds(0, total - rows)]
-    got(sent, q_sent)
-    got(sent, kv_sent.at[0])
-    got(sent, kv_sent.at[1])
+        got(early, q_sent.at[0])
+
+    @pl.when(jnp.logical_not(clean))
+    def _():
+        got(early, k_sent.at[0])
+        got(early, v_sent.at[0])
+
+    for sent in (q_sent, k_sent, v_sent):
+        got(late, sent.at[1])
     for which in range(2):
-        for tree in range(3):
-            place = kc.at[pl.ds(0, PART_ROWS[tree])]
-            for way in range(3):
-
-                @pl.when(passes(tree, way))
-                def _():
-                    got(place, c_sent.at[which, tree, way])
+        got(others, c_sent.at[which])
+
+        @pl.when(jnp.logical_and(clean, jnp.logical_not(own_holder)))
+        def _():
+            got(qh.at[pl.ds(0, rows)], first_sent.at[which])
 
     latent_copy.wait()
     got(mine, o_sent)
@@ -332,16 +355,20 @@
             pltpu.VMEM((1, 128), jnp.float32),
             pltpu.VMEM((total, 128), half),
             dma((6,)),
-            dma,
+            dma((2,)),
+            dma((2,)),
+            dma((2,)),
             dma((total // BLOCK,)),
             dma((2,)),
             dma((2,)),
-            dma((2, 3, 3)),
-            dma((2, 3, PARTS)),
+            dma((2,)),
+            dma((2,)),
+            dma((2,)),
             dma,
             dma,
             dma,
             dma,
+            pltpu.SemaphoreType.REGULAR,
             pltpu.SemaphoreType.REGULAR,
         ],
         compiler_params=pltpu.CompilerParams(

time: 226 us -> 94 us (0.42)
  the two profiles are of different devices: /device:TPU:23 before, /device:TPU:1 now
where the time goes in v2:
time: 94 us; the launch traced here: 93.9 us
  Pallas kernels  91.7 us (98%)
  other arithmetic  2.12 us (2%)
    pallas_call x1, Pallas kernels, body(): pl.pallas_call(kernel, out_shape=[jax.ShapeDtypeStruct((rows, width), hal...  91.7 us
    broadcast_in_dim x1, other arithmetic, body(): return advanced[None]  2.12 us

profile of v2, /device:TPU:1, one launch (start us, length us, event | category | flops | bytes accessed | tf_op | source)
XLA Modules:
  0.0 93.9 jit_solution(15852675516217983968)
XLA Ops:
  0.0 91.7 %shard_map.109 = (bf16[64,4096]{1,0:T(8,128)(2,1)}, bf16[64,4096]{1,0:T(8,128)(2,1)}) custom-call(s32[8]{0:T(128)} %times_ref.1, s32[8]{0:T(128)} %spans_ref.1, s32[8]{0:T(128)} %prefix_ref.1, f32[136,128]{1,0:T(8,128)} %constant.2.clone.freq_ref, bf16[64,4096]{1,0:T(8,128)(2,1)} %bitcast.6, bf16[64,4096]{1,0:T(8,128)(2,1)} %bitcast.7, ...), custom_call_target="tpu_custom_call" | custom-call | tf_op jit(solution)/shard_map/pallas_call | solution.py:334
  91.7 2.1 %fusion = bf16[1,64,4096]{2,1,0:T(8,128)(2,1)} fusion(bf16[64,4096]{1,0:T(8,128)(2,1)} %get-tuple-element.8, bf16[64,4096]{1,0:T(8,128)(2,1)} %get-tuple-element.7), kind=kLoop, calls=%fused_computation.1 | loop fusion | flops 1048576 | bytes 1572864 | tf_op jit(solution)/shard_map/broadcast_in_dim | solution.py:379

commit v3 on v2

--- a/solution.py
+++ b/solution.py
@@ -184,7 +184,6 @@
     @pl.when(jnp.logical_not(clean))
     def _():
         send_q()
-        got(early, q_sent.at[0])
         send_k()
         send_v()
 
@@ -192,11 +191,11 @@
     def _():
         pl.semaphore_wait(all_in, groups - 1)
         send_clean(lambda t: k_out.at[t], kc, k_sent, 0)
+        send_clean(v_of, vc, v_sent, 1)
+        send_q()
         got(early, k_sent.at[0])
-        send_clean(v_of, vc, v_sent, 1)
+        got(early, v_sent.at[0])
         hand_on(kc, 0)
-        got(early, v_sent.at[0])
-        send_q()
         hand_on(vc, 1)
 
     latent_copy = pltpu.make_async_remote_copy(
@@ -238,8 +237,8 @@
         return state
 
     def step(i, _):
-        first = jnp.where(clean, lax.rem(i, 2) == 0, i < blocks)
-        count = jnp.where(clean, lax.div(i, 2), lax.rem(i, blocks))
+        first = i < blocks
+        count = lax.rem(i, blocks)
         block = lax.rem(my_block + 2 * blocks - 1 - count, blocks)
         here = pl.ds(pl.multiple_of(block * BLOCK, BLOCK), BLOCK)
 
@@ -251,7 +250,7 @@
         def _():
             hand_on(vc, 1)
 
-        @pl.when(i == jnp.where(clean, 1, blocks))
+        @pl.when(i == blocks)
         def _():
             pl.semaphore_wait(next_in, 1)
             got(others, c_got.at[0])
@@ -308,6 +307,10 @@
     def _():
         got(early, k_sent.at[0])
         got(early, v_sent.at[0])
+
+    @pl.when(jnp.logical_not(clean))
+    def _():
+        got(early, q_sent.at[0])
 
     for sent in (q_sent, k_sent, v_sent):
         got(late, sent.at[1])

time: 94 us -> 85.6 us (0.911)
  the two profiles are of different devices: /device:TPU:1 before, /device:TPU:27 now
where the time goes in v3:
time: 85.6 us; the launch traced here: 85.5 us
  Pallas kernels  83.4 us (97%)
  other arithmetic  2.12 us (2%)
    pallas_call x1, Pallas kernels, body(): pl.pallas_call(kernel, out_shape=[jax.ShapeDtypeStruct((rows, width), hal...  83.4 us
    broadcast_in_dim x1, other arithmetic, body(): return advanced[None]  2.12 us

profile of v3, /device:TPU:27, one launch (start us, length us, event | category | flops | bytes accessed | tf_op | source)
XLA Modules:
  0.0 85.5 jit_solution(5335136267331196559)
XLA Ops:
  0.0 83.4 %shard_map.109 = (bf16[64,4096]{1,0:T(8,128)(2,1)}, bf16[64,4096]{1,0:T(8,128)(2,1)}) custom-call(s32[8]{0:T(128)} %times_ref.1, s32[8]{0:T(128)} %spans_ref.1, s32[8]{0:T(128)} %prefix_ref.1, f32[136,128]{1,0:T(8,128)} %constant.2.clone.freq_ref, bf16[64,4096]{1,0:T(8,128)(2,1)} %bitcast.6, bf16[64,4096]{1,0:T(8,128)(2,1)} %bitcast.7, ...), custom_call_target="tpu_custom_call" | custom-call | tf_op jit(solution)/shard_map/pallas_call | solution.py:337
  83.4 2.1 %fusion = bf16[1,64,4096]{2,1,0:T(8,128)(2,1)} fusion(bf16[64,4096]{1,0:T(8,128)(2,1)} %get-tuple-element.8, bf16[64,4096]{1,0:T(8,128)(2,1)} %get-tuple-element.7), kind=kLoop, calls=%fused_computation.1 | loop fusion | flops 1048576 | bytes 1572864 | tf_op jit(solution)/shard_map/broadcast_in_dim | solution.py:382

commit v4 on v3

--- a/solution.py
+++ b/solution.py
@@ -237,7 +237,7 @@
         return state
 
     def step(i, _):
-        first = i < blocks
+        first, final = i < blocks, i >= 2 * blocks
         count = lax.rem(i, blocks)
         block = lax.rem(my_block + 2 * blocks - 1 - count, blocks)
         here = pl.ds(pl.multiple_of(block * BLOCK, BLOCK), BLOCK)
@@ -250,16 +250,16 @@
         def _():
             hand_on(vc, 1)
 
-        @pl.when(i == blocks)
+        @pl.when(jnp.logical_and(jnp.logical_not(clean), i == blocks))
+        def _():
+            got(kh, kv_got.at[0])
+            got(vh, kv_got.at[1])
+
+        @pl.when(i == 2 * blocks)
         def _():
             pl.semaphore_wait(next_in, 1)
             got(others, c_got.at[0])
             got(others, c_got.at[1])
-
-        @pl.when(jnp.logical_and(jnp.logical_not(clean), i == blocks))
-        def _():
-            got(kh, kv_got.at[0])
-            got(vh, kv_got.at[1])
 
         @pl.when(first)
         def _():
@@ -270,19 +270,17 @@
             acc[here, :] = mixed
             peak[here, :] = jnp.broadcast_to(top, (BLOCK, 128))
 
-        @pl.when(jnp.logical_not(first))
+        @pl.when(jnp.logical_not(jnp.logical_or(jnp.logical_or(first, final), clean)))
         def _():
             q = qh[here, :]
-            top, mixed = attend((peak[here, 0:1], acc[here, :]), q, kc, vc, 0, total, False)
+            top, mixed = attend((peak[here, 0:1], acc[here, :]), q, kh, vh, 0, total, False)
             acc[here, :] = mixed
             peak[here, :] = jnp.broadcast_to(top, (BLOCK, 128))
 
-            @pl.when(jnp.logical_not(clean))
-            def _():
-                _, mixed = attend((peak[here, 0:1], acc[here, :]), q, kh, vh, 0, total, False)
-                acc[here, :] = mixed
-
-            mixed = acc[here, :]
+        @pl.when(final)
+        def _():
+            q = qh[here, :]
+            _, mixed = attend((peak[here, 0:1], acc[here, :]), q, kc, vc, 0, total, False)
             mine[here, :] = (mixed[:, :128] / mixed[:, 128:] * gate[...]).astype(jnp.bfloat16)
             for s in range(per):
                 owner = block * per + s
@@ -297,7 +295,7 @@
 
         return 0
 
-    lax.fori_loop(0, 2 * blocks, step, 0)
+    lax.fori_loop(0, 3 * blocks, step, 0)
 
     @pl.when(clean)
     def _():

time: 85.6 us -> 81.5 us (0.952)
  the two profiles are of different devices: /device:TPU:27 before, /device:TPU:1 now
where the time goes in v4:
time: 81.5 us; the launch traced here: 81.3 us
  Pallas kernels  79.2 us (97%)
  other arithmetic  2.12 us (3%)
    pallas_call x1, Pallas kernels, body(): pl.pallas_call(kernel, out_shape=[jax.ShapeDtypeStruct((rows, width), hal...  79.2 us
    broadcast_in_dim x1, other arithmetic, body(): return advanced[None]  2.12 us

profile of v4, /device:TPU:1, one launch (start us, length us, event | category | flops | bytes accessed | tf_op | source)
XLA Modules:
  0.0 81.3 jit_solution(3270045873185823242)
XLA Ops:
  0.0 79.2 %shard_map.109 = (bf16[64,4096]{1,0:T(8,128)(2,1)}, bf16[64,4096]{1,0:T(8,128)(2,1)}) custom-call(s32[8]{0:T(128)} %times_ref.1, s32[8]{0:T(128)} %spans_ref.1, s32[8]{0:T(128)} %prefix_ref.1, f32[136,128]{1,0:T(8,128)} %constant.2.clone.freq_ref, bf16[64,4096]{1,0:T(8,128)(2,1)} %bitcast.6, bf16[64,4096]{1,0:T(8,128)(2,1)} %bitcast.7, ...), custom_call_target="tpu_custom_call" | custom-call | tf_op jit(solution)/shard_map/pallas_call | solution.py:335
  79.2 2.1 %fusion = bf16[1,64,4096]{2,1,0:T(8,128)(2,1)} fusion(bf16[64,4096]{1,0:T(8,128)(2,1)} %get-tuple-element.8, bf16[64,4096]{1,0:T(8,128)(2,1)} %get-tuple-element.7), kind=kLoop, calls=%fused_computation.1 | loop fusion | flops 1048576 | bytes 1572864 | tf_op jit(solution)/shard_map/broadcast_in_dim | solution.py:380

commit v5 on v4

--- a/solution.py
+++ b/solution.py
@@ -181,6 +181,11 @@
     early = qh.at[pl.ds(0, EARLY * rows)]
     late = qh.at[pl.ds(0, (width - 1 - EARLY) * rows)]
 
+    latent_copy = pltpu.make_async_remote_copy(
+        latent_ref, moved_ref, l_sent, l_got, device_id={"step": after}, device_id_type=MESH
+    )
+    latent_copy.start()
+
     @pl.when(jnp.logical_not(clean))
     def _():
         send_q()
@@ -197,11 +202,6 @@
         got(early, v_sent.at[0])
         hand_on(kc, 0)
         hand_on(vc, 1)
-
-    latent_copy = pltpu.make_async_remote_copy(
-        latent_ref, moved_ref, l_sent, l_got, device_id={"step": after}, device_id_type=MESH
-    )
-    latent_copy.start()
 
     loads[3].wait()
     turns = times_ref[g].astype(jnp.float32) * freq[0:128, :]

time: 81.5 us -> 80.6 us (0.989); the launches traced: 81.3 us -> 79.1 us
  Pallas kernels: 79.2 us -> 76.9 us
    pallas_call x1, Pallas kernels: 79.2 us -> 76.9 us  [body(): pl.pallas_call(kernel, out_shape=[jax.ShapeDtypeStruct((rows, width), hal...]
where the time goes in v5:
time: 80.6 us; the launch traced here: 79.1 us
  Pallas kernels  76.9 us (95%)
  other arithmetic  2.12 us (3%)
    pallas_call x1, Pallas kernels, body(): pl.pallas_call(kernel, out_shape=[jax.ShapeDtypeStruct((rows, width), hal...  76.9 us
    broadcast_in_dim x1, other arithmetic, body(): return advanced[None]  2.12 us

profile of v5, /device:TPU:1, one launch (start us, length us, event | category | flops | bytes accessed | tf_op | source)
XLA Modules:
  0.0 79.1 jit_solution(7609298604567033956)
XLA Ops:
  0.0 76.9 %shard_map.109 = (bf16[64,4096]{1,0:T(8,128)(2,1)}, bf16[64,4096]{1,0:T(8,128)(2,1)}) custom-call(s32[8]{0:T(128)} %times_ref.1, s32[8]{0:T(128)} %spans_ref.1, s32[8]{0:T(128)} %prefix_ref.1, f32[136,128]{1,0:T(8,128)} %constant.2.clone.freq_ref, bf16[64,4096]{1,0:T(8,128)(2,1)} %bitcast.6, bf16[64,4096]{1,0:T(8,128)(2,1)} %bitcast.7, ...), custom_call_target="tpu_custom_call" | custom-call | tf_op jit(solution)/shard_map/pallas_call | solution.py:335
  76.9 2.1 %fusion = bf16[1,64,4096]{2,1,0:T(8,128)(2,1)} fusion(bf16[64,4096]{1,0:T(8,128)(2,1)} %get-tuple-element.8, bf16[64,4096]{1,0:T(8,128)(2,1)} %get-tuple-element.7), kind=kLoop, calls=%fused_computation.1 | loop fusion | flops 1048576 | bytes 1572864 | tf_op jit(solution)/shard_map/broadcast_in_dim | solution.py:380
